TPU v7x, 32 devices: a whole 2x2x4 slice. The times are simulated.
32 devices in a mesh: groups: 2 (over y), row: 4 (over x, core), col: 4 (over z).
Axes of the slice: x: 2, y: 2, z: 4, core: 2. Of those that a mesh axis runs over, the one named last changes fastest.
Arguments:
- tokens: bfloat16 [512, 8192], P(('groups', 'col'), 'row'), parts along dimension 0, may hold values from -6 to 6
- gate_weight: bfloat16 [8192, 14336], P('row', 'col'), may hold values from -0.0625 to 0.0625
- up_weight: bfloat16 [8192, 14336], P('row', 'col'), may hold values from -0.0625 to 0.0625
- down_weight: bfloat16 [14336, 8192], P('col', 'row'), may hold values from -0.046875 to 0.046875
- gate_left: bfloat16 [16384, 512], P(('groups', 'row'), 'col'), parts along dimension 0, may hold values from -0.25 to 0.25
- gate_right: bfloat16 [1024, 14336], P(('groups', 'row'), 'col'), parts along dimension 0, may hold values from -0.0625 to 0.0625
- up_left: bfloat16 [16384, 512], P(('groups', 'row'), 'col'), parts along dimension 0, may hold values from -0.25 to 0.25
- up_right: bfloat16 [1024, 14336], P(('groups', 'row'), 'col'), parts along dimension 0, may hold values from -0.0625 to 0.0625
- down_left: bfloat16 [28672, 512], P(('groups', 'col'), 'row'), parts along dimension 0, may hold values from -0.25 to 0.25
- down_right: bfloat16 [1024, 8192], P(('groups', 'col'), 'row'), parts along dimension 0, may hold values from -0.046875 to 0.046875
Outputs:
- mixed: bfloat16 [512, 8192], P(('groups', 'col'), 'row'), parts along dimension 0
- gate_merged: bfloat16 [16384, 14336], P(('groups', 'row'), 'col'), parts along dimension 0
- up_merged: bfloat16 [16384, 14336], P(('groups', 'row'), 'col'), parts along dimension 0
- down_merged: bfloat16 [28672, 8192], P(('groups', 'col'), 'row'), parts along dimension 0
There are 2 independent parts, one for each index of `groups`. A program takes and returns all parts, laid end to end along the dimension named above; an argument that names none is the same for every part. Nothing has to cross between parts.
All inputs are finite; a program needn't handle non-finite values.
Results may differ from a plain program's by a relative error of at most 0.007.
Values may be sent and summed in bfloat16 or wider, within the bound.
A program may use at most 256 MiB of HBM per device.

v0:
```python
import jax
import jax.numpy as jnp
from jax import lax
from jax.sharding import PartitionSpec as P


def merge_delta(weight, left, right):
    delta = jnp.dot(left, right, preferred_element_type=jnp.float32)
    return (weight.astype(jnp.float32) + delta).astype(jnp.bfloat16)


def local(
    tokens,
    gate_weight,
    up_weight,
    down_weight,
    gate_left,
    gate_right,
    up_left,
    up_right,
    down_left,
    down_right,
):
    gate_full_left, up_full_left, down_full_right = (
        lax.all_gather(gate_left, "col", axis=1, tiled=True),
        lax.all_gather(up_left, "col", axis=1, tiled=True),
        lax.all_gather(down_right, "col", axis=0, tiled=True),
    )
    gate_full_right, up_full_right, down_full_left = (
        lax.all_gather(gate_right, "row", axis=0, tiled=True),
        lax.all_gather(up_right, "row", axis=0, tiled=True),
        lax.all_gather(down_left, "row", axis=1, tiled=True),
    )
    gate_merged = merge_delta(gate_weight, gate_full_left, gate_full_right)
    up_merged = merge_delta(up_weight, up_full_left, up_full_right)
    down_merged = merge_delta(down_weight, down_full_left, down_full_right)
    joined = jnp.concatenate([gate_merged, up_merged], axis=1)
    width = gate_merged.shape[1]
    partial_terms = jnp.dot(
        lax.all_gather(tokens, "col", axis=0, tiled=True),
        joined,
        preferred_element_type=jnp.float32,
    )
    share = lax.psum_scatter(partial_terms, "row", scatter_dimension=0, tiled=True)
    local_hidden = (jax.nn.silu(share[:, :width]) * share[:, width:]).astype(jnp.bfloat16)
    hidden = lax.all_gather(local_hidden, "row", axis=0, tiled=True)
    mixed = lax.psum_scatter(
        jnp.dot(hidden, down_merged, preferred_element_type=jnp.float32),
        "col",
        scatter_dimension=0,
        tiled=True,
    )
    return (mixed.astype(jnp.bfloat16), gate_merged, up_merged, down_merged)


def solution(mesh):
    in_specs = (
        P(("groups", "col"), "row"),
        P("row", "col"),
        P("row", "col"),
        P("col", "row"),
        P(("groups", "row"), "col"),
        P(("groups", "row"), "col"),
        P(("groups", "row"), "col"),
        P(("groups", "row"), "col"),
        P(("groups", "col"), "row"),
        P(("groups", "col"), "row"),
    )
    out_specs = (
        P(("groups", "col"), "row"),
        P(("groups", "row"), "col"),
        P(("groups", "row"), "col"),
        P(("groups", "col"), "row"),
    )
    return jax.shard_map(local, mesh=mesh, in_specs=in_specs, out_specs=out_specs, check_vma=False)
```

profile of v0, /device:TPU:0, one launch (start us, length us, event | category | flops | bytes accessed | tf_op | source)
XLA Modules:
  0.0 454.2 jit_solution(13828735019121942896)
XLA Ops:
  7.2 0.7 all-gather.13.cloned.1.call-update
  7.9 0.7 all-gather.15.cloned.1.call-update
  8.7 0.7 all-gather.9.cloned.1.call-update
  10.0 0.5 all-gather.17.cloned.1.call-update
  10.6 47.9 %all-gather.13.cloned.1.call-done = bf16[2048,512]{1,0:T(8,128)(2,1)} async-done(((bf16[2048,128]{1,0:T(8,128)(2,1)}), bf16[2048,512]{1,0:T(8,128)(2,1)}) %all-gather.13.cloned.1.call-update) | async-done | bytes 2097168 | tf_op jit(solution)/shard_map/all_gather | solution.py:26
  58.5 31.3 %all-gather.15.cloned.1.call-done = bf16[512,3584]{1,0:T(8,128)(2,1)} async-done(((bf16[128,3584]{1,0:T(8,128)(2,1)}), bf16[512,3584]{1,0:T(8,128)(2,1)}) %all-gather.15.cloned.1.call-update) | async-done | bytes 3670032 | tf_op jit(solution)/shard_map/all_gather | solution.py:31
  89.9 15.3 %add_convert_fusion.1 = bf16[2048,3584]{1,0:T(8,128)(2,1)} fusion(bf16[2048,3584]{1,0:T(8,128)(2,1)} %param.12, bf16[2048,512]{1,0:T(8,128)(2,1)} %all-gather.13.cloned.1.call-done, bf16[512,3584]{1,0:T(8,128)(2,1)} %all-gather.15.cloned.1.call-done), kind=kOutput, calls=%fused_computation.5 | convolution fusion | flops 7538212864 | bytes 35127296 | tf_op jit(solution)/shard_map/dot_general | solution.py:8
  105.2 32.5 %all-gather.9.cloned.1.call-done = bf16[2048,512]{1,0:T(8,128)(2,1)} async-done(((bf16[2048,128]{1,0:T(8,128)(2,1)}), bf16[2048,512]{1,0:T(8,128)(2,1)}) %all-gather.9.cloned.1.call-update) | async-done | bytes 2097168 | tf_op jit(solution)/shard_map/all_gather | solution.py:25
  137.7 31.2 %all-gather.11.cloned.1.call-done = bf16[512,3584]{1,0:T(8,128)(2,1)} async-done(((bf16[128,3584]{1,0:T(8,128)(2,1)}), bf16[512,3584]{1,0:T(8,128)(2,1)}) %all-gather.11.cloned.1.call-update) | async-done | bytes 3670032 | tf_op jit(solution)/shard_map/all_gather | solution.py:30
  168.9 15.4 %add_convert_fusion.2 = bf16[2048,3584]{1,0:T(8,128)(2,1)} fusion(bf16[2048,3584]{1,0:T(8,128)(2,1)} %param.11, bf16[2048,512]{1,0:T(8,128)(2,1)} %all-gather.9.cloned.1.call-done, bf16[512,3584]{1,0:T(8,128)(2,1)} %all-gather.11.cloned.1.call-done), kind=kOutput, calls=%fused_computation.6 | convolution fusion | flops 7538212864 | bytes 35127296 | tf_op jit(solution)/shard_map/dot_general | solution.py:8
  184.3 14.0 %all-gather.17.cloned.1.call-done = bf16[256,2048]{1,0:T(8,128)(2,1)} async-done(((bf16[64,2048]{1,0:T(8,128)(2,1)}), bf16[256,2048]{1,0:T(8,128)(2,1)}) %all-gather.17.cloned.1.call-update) | async-done | bytes 1048592 | tf_op jit(solution)/shard_map/all_gather | solution.py:40
  198.3 16.0 %fusion.4 = f32[256,7168]{0,1:T(8,128)} fusion(bf16[256,2048]{1,0:T(8,128)(2,1)} %all-gather.17.cloned.1.call-done, bf16[2048,3584]{1,0:T(8,128)(2,1)} %add_convert_fusion.1, bf16[2048,3584]{1,0:T(8,128)(2,1)} %add_convert_fusion.2), kind=kOutput, calls=%fused_computation.7 | convolution fusion | flops 7574913024 | bytes 37748736 | tf_op jit(solution)/shard_map/dot_general | solution.py:39
  214.2 8.4 %copy.17 = f32[256,7168]{1,0:T(8,128)} copy(f32[256,7168]{0,1:T(8,128)} %fusion.4) | data formatting | bytes 14680064
  222.7 0.7 all-gather.23.cloned.1.call-update
  223.5 0.7 all-gather.21.cloned.1.call-update
  224.2 63.5 %reduce-scatter.7.cloned.1.call-done = f32[64,7168]{1,0:T(8,128)} async-done(((f32[256,7168]{1,0:T(8,128)}), f32[64,7168]{1,0:T(8,128)}) %reduce-scatter.7.cloned.1.call-update) | async-done | bytes 1835024 | tf_op jit(solution)/shard_map/reduce_scatter | solution.py:44
  287.7 2.5 fusion.7
  290.5 44.9 %all-gather.23.cloned.1.call-done = bf16[512,2048]{1,0:T(8,128)(2,1)} async-done(((bf16[128,2048]{1,0:T(8,128)(2,1)}), bf16[512,2048]{1,0:T(8,128)(2,1)}) %all-gather.23.cloned.1.call-update) | async-done | bytes 2097168 | tf_op jit(solution)/shard_map/all_gather | solution.py:27
  335.4 32.3 %all-gather.21.cloned.1.call-done = bf16[3584,512]{1,0:T(8,128)(2,1)} async-done(((bf16[3584,128]{1,0:T(8,128)(2,1)}), bf16[3584,512]{1,0:T(8,128)(2,1)}) %all-gather.21.cloned.1.call-update) | async-done | bytes 3670032 | tf_op jit(solution)/shard_map/all_gather | solution.py:32
  367.7 15.3 %add_convert_fusion = bf16[3584,2048]{1,0:T(8,128)(2,1)} fusion(bf16[3584,2048]{1,0:T(8,128)(2,1)} %param.13, bf16[3584,512]{1,0:T(8,128)(2,1)} %all-gather.21.cloned.1.call-done, bf16[512,2048]{1,0:T(8,128)(2,1)} %all-gather.23.cloned.1.call-done), kind=kOutput, calls=%fused_computation.4 | convolution fusion | flops 7538212864 | bytes 35127296 | tf_op jit(solution)/shard_map/dot_general | solution.py:8
  383.0 7.5 %all-gather.19.cloned.1.call-done = bf16[256,3584]{1,0:T(8,128)(2,1)} async-done(((bf16[64,3584]{1,0:T(8,128)(2,1)}), bf16[256,3584]{1,0:T(8,128)(2,1)}) %all-gather.19.cloned.1.call-update) | async-done | bytes 1835024 | tf_op jit(solution)/shard_map/all_gather | solution.py:46
  390.5 11.0 %fusion.9 = f32[256,2048]{1,0:T(8,128)} fusion(bf16[256,3584]{1,0:T(8,128)(2,1)} %all-gather.19.cloned.1.call-done, bf16[3584,2048]{1,0:T(8,128)(2,1)} %add_convert_fusion), kind=kOutput, calls=%fused_computation.11 | convolution fusion | flops 3758096384 | bytes 18612224 | tf_op jit(solution)/shard_map/dot_general | solution.py:48
  401.6 44.0 %reduce-scatter.5.cloned.1.call-done = f32[64,2048]{1,0:T(8,128)} async-done(((f32[256,2048]{1,0:T(8,128)}), f32[64,2048]{1,0:T(8,128)}) %reduce-scatter.5.cloned.1.call-update) | async-done | bytes 524304 | tf_op jit(solution)/shard_map/reduce_scatter | solution.py:47
  445.6 1.8 convert_element_type.31
  (14 shorter events, 1.1 us)
Async XLA Ops:
  7.2 51.4 %all-gather.13.cloned.1.call-start = ((), (), s32[]{:S(2)}) async-start(), calls=%async_computation.4 | async-start | bytes 2621440 | tf_op jit(solution)/shard_map/all_gather | solution.py:26
  7.9 82.0 %all-gather.15.cloned.1.call-start = ((), (), s32[]{:S(2)}) async-start(), calls=%async_computation.5 | async-start | bytes 4587520 | tf_op jit(solution)/shard_map/all_gather | solution.py:31
  8.6 129.1 %all-gather.9.cloned.1.call-start = ((), (), s32[]{:S(2)}) async-start(), calls=%async_computation.2 | async-start | bytes 2621440 | tf_op jit(solution)/shard_map/all_gather | solution.py:25
  9.4 159.5 %all-gather.11.cloned.1.call-start = ((), (), s32[]{:S(2)}) async-start(), calls=%async_computation.3 | async-start | bytes 4587520 | tf_op jit(solution)/shard_map/all_gather | solution.py:30
  10.0 188.3 %all-gather.17.cloned.1.call-start = ((), (), s32[]{:S(2)}) async-start(), calls=%async_computation.6 | async-start | bytes 1310720 | tf_op jit(solution)/shard_map/all_gather | solution.py:40
  10.5 277.2 %reduce-scatter.7.cloned.1.call-start = ((), (), s32[]{:S(2)}) async-start(), calls=%async_computation.11 | async-start | bytes 9175040 | tf_op jit(solution)/shard_map/reduce_scatter | solution.py:44
  222.7 112.7 %all-gather.23.cloned.1.call-start = ((), (), s32[]{:S(2)}) async-start(), calls=%async_computation.9 | async-start | bytes 2621440 | tf_op jit(solution)/shard_map/all_gather | solution.py:27
  223.4 144.3 %all-gather.21.cloned.1.call-start = ((), (), s32[]{:S(2)}) async-start(), calls=%async_computation.8 | async-start | bytes 4587520 | tf_op jit(solution)/shard_map/all_gather | solution.py:32
  224.2 166.4 %all-gather.19.cloned.1.call-start = ((), (), s32[]{:S(2)}) async-start(), calls=%async_computation.7 | async-start | bytes 2293760 | tf_op jit(solution)/shard_map/all_gather | solution.py:46
  290.2 155.4 %reduce-scatter.5.cloned.1.call-start = ((), (), s32[]{:S(2)}) async-start(), calls=%async_computation.10 | async-start | bytes 2621440 | tf_op jit(solution)/shard_map/reduce_scatter | solution.py:47
Sparse Core Ops, SparseCore 0:
  9.6 48.9 all-gather.12
  60.1 29.7 all-gather.14
  91.4 46.2 all-gather.8
  139.1 29.7 all-gather.10
  170.3 27.9 all-gather.16
  222.8 64.9 reduce-scatter.6
  289.4 45.9 all-gather.22
  337.0 30.6 all-gather.20
  369.4 21.1 all-gather.18
  401.7 43.8 reduce-scatter.4
where the time goes:
time: 455 us; the launch traced here: 454 us
  waiting for transfers between devices  354 us (78%)
  matrix products  73 us (16%)
  between operations  14.2 us (3%)
  local copies, waits for them, and re-layouts  8.39 us (2%)
    reduce_scatter x1, waiting for transfers between devices, local(): lax.psum_scatter(partial_terms, 'row', scatter_dimension=0, tiled=True)  63.5 us
    all_gather x1, waiting for transfers between devices, local(): lax.all_gather(up_left, 'col', axis=1, tiled=True)  47.9 us
    dot_general x3, matrix products, merge_delta(): delta = jnp.dot(left, right, preferred_element_type=jnp.float32)  46 us
    all_gather x1, waiting for transfers between devices, local(): lax.all_gather(down_right, 'col', axis=0, tiled=True)  44.9 us
    reduce_scatter x1, waiting for transfers between devices, local(): lax.psum_scatter(jnp.dot(hidden, down_merged, preferred_element_type=jnp....  44 us
    all_gather x1, waiting for transfers between devices, local(): lax.all_gather(gate_left, 'col', axis=1, tiled=True)  32.5 us
    all_gather x1, waiting for transfers between devices, local(): lax.all_gather(down_left, 'row', axis=1, tiled=True)  32.3 us
    all_gather x1, waiting for transfers between devices, local(): lax.all_gather(up_right, 'row', axis=0, tiled=True)  31.3 us
  transfers between devices with their start and end apart: 10, of which 10 were waited for; matrix products, arithmetic and copies ran while one was open for 11% of the time, Pallas kernels for 0%

commit v1 on v0

v1 whole, which is shorter than its diff:
```python
import functools

import jax
import jax.numpy as jnp
from jax import lax
from jax.experimental import pallas as pl
from jax.experimental.pallas import tpu as pltpu
from jax.sharding import PartitionSpec as P

F32 = jnp.float32
BF16 = jnp.bfloat16


def put(whole, piece, slot, axis):
    start = [0] * whole.ndim
    start[axis] = slot * piece.shape[axis]
    return lax.dynamic_update_slice(whole, piece, start)


def take(whole, slot, size, axis=0):
    return lax.dynamic_slice_in_dim(whole, slot * size, size, axis)


def dot(a, b):
    return jnp.dot(a, b, preferred_element_type=F32)


def merge_delta(weight, left, right):
    return (weight.astype(F32) + dot(left, right)).astype(BF16)


def line_gather(x, axis, n):
    if n != 4:
        return lax.all_gather(x, "col", axis=axis, tiled=True)
    me = lax.axis_index("col")
    ups, downs = [x], [x]
    for step in range(1, n):
        ups.append(lax.ppermute(ups[-1], "col", [(i, i + 1) for i in range(step - 1, n - 1)]))
        downs.append(lax.ppermute(downs[-1], "col", [(i, i - 1) for i in range(1, n - step + 1)]))
    shape = list(x.shape)
    shape[axis] *= n
    whole = put(jnp.zeros(shape, x.dtype), x, me, axis)
    for step in range(1, n):
        piece = jnp.where(me >= step, ups[step], downs[n - step])
        whole = put(whole, piece, lax.rem(me - step + n, n), axis)
    return whole


def row_swap(x, bit):
    return lax.ppermute(x, "row", [(i, i ^ bit) for i in range(4)])


def row_gather(x, axis, n):
    if n != 4:
        return lax.all_gather(x, "row", axis=axis, tiled=True)
    me = lax.axis_index("row")
    far = row_swap(x, 2)
    near = row_swap(x, 1)
    corner = row_swap(far, 1)
    shape = list(x.shape)
    shape[axis] *= n
    whole = jnp.zeros(shape, x.dtype)
    for bit, piece in ((0, x), (1, near), (2, far), (3, corner)):
        whole = put(whole, piece, jnp.bitwise_xor(me, bit), axis)
    return whole


def row_scatter_sum(x, n):
    if n != 4:
        return lax.psum_scatter(x, "row", scatter_dimension=0, tiled=True)
    me = lax.axis_index("row")
    size = x.shape[0] // n
    blocks = x.reshape(2, 2, size, x.shape[1])
    core = me % 2
    kept = lax.dynamic_index_in_dim(blocks, core, 1, keepdims=False)
    given = lax.dynamic_index_in_dim(blocks, 1 - core, 1, keepdims=False)
    both = kept + row_swap(given, 1)
    chip = me // 2
    mine = lax.dynamic_index_in_dim(both, chip, 0, keepdims=False)
    other = lax.dynamic_index_in_dim(both, 1 - chip, 0, keepdims=False)
    return mine + row_swap(other.astype(BF16), 2).astype(F32)


def row_sum(x, n):
    if n != 4:
        return lax.psum(x, "row")
    x = x + row_swap(x, 1)
    return x + row_swap(x, 2)


def turn(x, step, n):
    return lax.ppermute(x, "col", [(i, (i + step) % n) for i in range(n)])


def col_sum(x, n):
    if n != 4:
        return lax.psum(x, "col")
    terms = [turn(x, step, n) for step in range(1, n)]
    for term in terms:
        x = x + term
    return x


def col_scatter_sum(x, n):
    if n != 4:
        return lax.psum_scatter(x, "col", scatter_dimension=0, tiled=True)
    me = lax.axis_index("col")
    size = x.shape[0] // n
    total = take(x, me, size)
    for step in range(1, n):
        block = take(x, lax.rem(me + step, n), size).astype(BF16)
        total = total + turn(block, step, n).astype(F32)
    return total


def gather_kernel(lines, rows, *refs):
    total = len(lines) + len(rows)
    ins, outs = refs[:total], refs[total : 2 * total]
    own_sem, send_sem, recv_sem = refs[2 * total :]
    n = 4
    col, row = lax.axis_index("col"), lax.axis_index("row")
    dims = lines + rows

    barrier = pltpu.get_barrier_semaphore()
    for target in (
        {"col": lax.rem(col + 1, n)},
        {"col": lax.rem(col + n - 1, n)},
        {"row": jnp.bitwise_xor(row, 1)},
        {"row": jnp.bitwise_xor(row, 2)},
    ):
        pl.semaphore_signal(barrier, inc=1, device_id=target, device_id_type=pl.DeviceIdType.MESH)
    pl.semaphore_wait(barrier, 4)

    def view(t, slot):
        size = ins[t].shape[dims[t]]
        part = pl.ds(pl.multiple_of(slot * size, size), size)
        return outs[t].at[part, :] if dims[t] == 0 else outs[t].at[:, part]

    def send(t, slot, first, order, target):
        return pltpu.make_async_remote_copy(
            src_ref=ins[t] if first else view(t, slot),
            dst_ref=view(t, slot),
            send_sem=send_sem.at[t, order],
            recv_sem=recv_sem.at[t, slot],
            device_id=target,
            device_id_type=pl.DeviceIdType.MESH,
        )

    def own(t):
        return pltpu.make_async_copy(ins[t], view(t, col if t < len(lines) else row), own_sem.at[t])

    def relay(t, step, way, act):
        slot, target = col - way * step, col + way
        inside = (slot >= 0) & (slot < n) & (target >= 0) & (target < n)

        @pl.when(inside)
        def _():
            copy = send(t, slot, step == 0, step if way > 0 else 3 + step, {"col": target})
            if act == "wait":
                copy.wait_send()
            else:
                copy.start()

    def arrive(t, step, way):
        slot = col - way * step

        @pl.when((slot >= 0) & (slot < n))
        def _():
            send(t, slot, False, 0, {"col": col}).wait_recv()

    def row_copy(t, order):
        near, far = {"row": jnp.bitwise_xor(row, 1)}, {"row": jnp.bitwise_xor(row, 2)}
        if order == 0:
            return send(t, row, True, 0, far)
        if order == 1:
            return send(t, row, True, 1, near)
        return send(t, jnp.bitwise_xor(row, 2), False, 2, near)

    on_line, on_row = range(len(lines)), range(len(lines), total)
    for t in on_line:
        for way in (1, -1):
            relay(t, 0, way, "start")
    for t in on_row:
        row_copy(t, 0).start()
        row_copy(t, 1).start()
    for t in range(total):
        own(t).start()

    passing = [(t, step) for step in range(1, n) for t in on_line]
    crossing = list(on_row)
    for place, (t, step) in enumerate(passing):
        for way in (1, -1):
            arrive(t, step, way)
            if step < n - 1:
                relay(t, step, way, "start")
        if crossing and place % 2 == 1:
            t = crossing.pop(0)
            send(t, jnp.bitwise_xor(row, 2), False, 0, {"row": row}).wait_recv()
            row_copy(t, 2).start()
    for t in crossing:
        send(t, jnp.bitwise_xor(row, 2), False, 0, {"row": row}).wait_recv()
        row_copy(t, 2).start()
    for t in on_row:
        for bit in (1, 3):
            send(t, jnp.bitwise_xor(row, bit), False, 0, {"row": row}).wait_recv()
        for order in range(3):
            row_copy(t, order).wait_send()
    for t in on_line:
        for way in (1, -1):
            for step in range(n - 1):
                relay(t, step, way, "wait")
    for t in range(total):
        own(t).wait()


def gather_all(nrow, ncol, lines, rows):
    if nrow != 4 or ncol != 4:
        done = [lax.all_gather(x, "col", axis=axis, tiled=True) for x, axis in lines]
        return done + [lax.all_gather(x, "row", axis=axis, tiled=True) for x, axis in rows]
    shapes = []
    for x, axis in lines + rows:
        shape = list(x.shape)
        shape[axis] *= 4
        shapes.append(jax.ShapeDtypeStruct(tuple(shape), x.dtype))
    total = len(shapes)
    moved = sum(s.size * 2 for s in shapes)
    return pl.pallas_call(
        functools.partial(gather_kernel, tuple(a for _, a in lines), tuple(a for _, a in rows)),
        out_shape=shapes,
        in_specs=[pl.BlockSpec(memory_space=pl.ANY)] * total,
        out_specs=[pl.BlockSpec(memory_space=pl.ANY)] * total,
        scratch_shapes=[
            pltpu.SemaphoreType.DMA((total,)),
            pltpu.SemaphoreType.DMA((total, 6)),
            pltpu.SemaphoreType.DMA((total, 4)),
        ],
        compiler_params=pltpu.CompilerParams(collective_id=0, has_side_effects=True),
        cost_estimate=pl.CostEstimate(flops=0, bytes_accessed=moved, transcendentals=0),
    )(*[x for x, _ in lines + rows])


def local(
    nrow,
    ncol,
    tokens,
    gate_weight,
    up_weight,
    down_weight,
    gate_left,
    gate_right,
    up_left,
    up_right,
    down_left,
    down_right,
):
    block, gate_l, up_l, gate_r, up_r, down_l = gather_all(
        nrow,
        ncol,
        [(tokens, 0), (gate_left, 1), (up_left, 1)],
        [(gate_right, 0), (up_right, 0), (down_left, 1)],
    )
    down_right, block = lax.optimization_barrier((down_right, block))
    down_r = lax.all_gather(down_right, "col", axis=0, tiled=True)

    def apply(x, weight, left, right):
        return dot(x, weight) + dot(dot(x, left).astype(BF16), right)

    gate = row_scatter_sum(apply(block, gate_weight, gate_l, gate_r), nrow)
    up = row_scatter_sum(apply(block, up_weight, up_l, up_r), nrow)
    hidden = row_gather((jax.nn.silu(gate) * up).astype(BF16), 0, nrow)
    mixed = col_scatter_sum(apply(hidden, down_weight, down_l, down_r), ncol)

    gate_merged = merge_delta(gate_weight, gate_l, gate_r)
    up_merged = merge_delta(up_weight, up_l, up_r)
    down_merged = merge_delta(down_weight, down_l, down_r)
    return (mixed.astype(BF16), gate_merged, up_merged, down_merged)


def solution(mesh):
    nrow, ncol = mesh.shape["row"], mesh.shape["col"]
    in_specs = (
        P(("groups", "col"), "row"),
        P("row", "col"),
        P("row", "col"),
        P("col", "row"),
        P(("groups", "row"), "col"),
        P(("groups", "row"), "col"),
        P(("groups", "row"), "col"),
        P(("groups", "row"), "col"),
        P(("groups", "col"), "row"),
        P(("groups", "col"), "row"),
    )
    out_specs = (
        P(("groups", "col"), "row"),
        P(("groups", "row"), "col"),
        P(("groups", "row"), "col"),
        P(("groups", "col"), "row"),
    )
    return jax.shard_map(
        lambda *a: local(nrow, ncol, *a), mesh=mesh, in_specs=in_specs, out_specs=out_specs, check_vma=False
    )
```

time: 455 us -> 274 us (0.60)
  waiting for transfers between devices: 354 us -> 9.63 us
  Pallas kernels: 0 us -> 130 us
  matrix products: 73 us -> 93.6 us
  starting transfers between devices: 0.57 us -> 9.03 us
    all_gather x8 -> x1, waiting for transfers between devices: 242 us -> 0.02 us  [local(): down_r = lax.all_gather(down_right, 'col', axis=0, tiled=True)]
    pallas_call x0 -> x1, Pallas kernels: none -> 130 us  [gather_all(): pl.pallas_call(functools.partial(gather_kernel, tuple((a for _, a in line...]
    reduce_scatter x2 -> x0, waiting for transfers between devices: 108 us -> none  [the longest x1 63.5 us: local(): lax.psum_scatter(partial_terms, 'row', scatter_dimension=0, tiled=True)]
    dot_general x5 -> x9, matrix products: 73 us -> 93.6 us  [dot(): return jnp.dot(a, b, preferred_element_type=F32)]
    ppermute x0 -> x10, waiting for transfers between devices: none -> 9.59 us  [the longest x3 6.41 us: turn(): return lax.ppermute(x, 'col', [(i, (i + step) % n) for i in range(n)])]
    ppermute x0 -> x10, starting transfers between devices: none -> 8.99 us  [the longest x7 5.12 us: row_swap(): return lax.ppermute(x, 'row', [(i, i ^ bit) for i in range(4)])]
    unnamed x1 -> x18, local copies, waits for them, and re-layouts: 8.39 us -> 2.52 us
    squeeze x0 -> x2, local copies, waits for them, and re-layouts: none -> 5.72 us  [row_scatter_sum(): given = lax.dynamic_index_in_dim(blocks, 1 - core, 1, keepdims=False)]
  transfers between devices with their start and end apart: 10 -> 11, of which waited for: 10 -> 3; matrix products, arithmetic and copies ran while one was open for 11% -> 26% of each run, Pallas kernels for 0% -> 0%
where the time goes in v1:
time: 274 us; the launch traced here: 273 us
  Pallas kernels  130 us (47%)
  matrix products  93.6 us (34%)
  between operations  14.3 us (5%)
  waiting for transfers between devices  9.63 us (4%)
  starting transfers between devices  9.03 us (3%)
  local copies, waits for them, and re-layouts  8.68 us (3%)
  other arithmetic  8.37 us (3%)
    pallas_call x1, Pallas kernels, gather_all(): pl.pallas_call(functools.partial(gather_kernel, tuple((a for _, a in line...  130 us
    dot_general x9, matrix products, dot(): return jnp.dot(a, b, preferred_element_type=F32)  93.6 us
    ppermute x3, waiting for transfers between devices, turn(): return lax.ppermute(x, 'col', [(i, (i + step) % n) for i in range(n)])  6.41 us
    squeeze x2, local copies, waits for them, and re-layouts, row_scatter_sum(): given = lax.dynamic_index_in_dim(blocks, 1 - core, 1, keepdims=False)  5.72 us
  transfers between devices with their start and end apart: 11, of which 3 were waited for; matrix products, arithmetic and copies ran while one was open for 26% of the time, Pallas kernels for 0%

profile of v1, /device:TPU:0, one launch (start us, length us, event | category | flops | bytes accessed | tf_op | source)
XLA Modules:
  0.0 273.5 jit_solution(11598623711733186289)
XLA Ops:
  7.2 129.9 %shard_map.129 = (bf16[256,2048]{1,0:T(8,128)(2,1)}, bf16[2048,512]{1,0:T(8,128)(2,1)}, bf16[2048,512]{1,0:T(8,128)(2,1)}, bf16[512,3584]{1,0:T(8,128)(2,1)}, bf...) custom-call(bf16[64,2048]{1,0:T(8,128)(2,1)} %refs_0_.1, bf16[2048,128]{1,0:T(8,128)(2,1)} %refs_1_.1, ...), custom_call_target="tpu_custom_call" | custom-call | bytes 16252928 | tf_op jit(solution)/shard_map/pallas_call | solution.py:227
  137.1 11.4 %fusion.7 = f32[256,3584]{1,0:T(8,128)} fusion(bf16[256,2048]{1,0:T(8,128)(2,1)} %get-tuple-element.13, bf16[2048,3584]{1,0:T(8,128)(2,1)} %param.12), kind=kOutput, calls=%fused_computation.31 | convolution fusion | flops 3758096384 | bytes 19398656 | tf_op jit(solution)/shard_map/dot_general | solution.py:25
  148.6 6.7 %convolution_add_fusion = f32[256,3584]{1,0:T(8,128)} fusion(f32[256,3584]{1,0:T(8,128)} %fusion.7, bf16[512,3584]{1,0:T(8,128)(2,1)} %get-tuple-element.17, bf16[256,2048]{1,0:T(8,128)(2,1)S(1)} %copy-done.3, bf16[2048,512]{1,0:T(8,128)(2,1)S(1)} %copy-done.5), kind=kOutput, calls=%fused_computation.3 | convolution fusion | flops 1477443584 | bytes 14155776 | tf_op jit(solution)/shard_map/dot_general | solution.py:25
  155.3 2.9 %dynamic-slice_bitcast_fusion = f32[2,64,3584]{2,1,0:T(8,128)} fusion(f32[2,2,64,3584]{3,2,1,0:T(8,128)} %bitcast.49, s32[]{:T(128)S(6)} %select_n.58), kind=kLoop, calls=%fused_computation.8 | loop fusion | bytes 3670020 | tf_op jit(solution)/shard_map/jit(dynamic_index_in_dim)/squeeze | solution.py:76
  158.2 9.2 %fusion.6 = f32[256,3584]{1,0:T(8,128)} fusion(bf16[256,2048]{1,0:T(8,128)(2,1)S(1)} %copy-done.3, bf16[2048,3584]{1,0:T(8,128)(2,1)} %param.11), kind=kOutput, calls=%fused_computation.30 | convolution fusion | flops 3758096384 | bytes 19398656 | tf_op jit(solution)/shard_map/dot_general | solution.py:25
  167.4 6.7 %convolution_add_fusion.1 = f32[256,3584]{1,0:T(8,128)} fusion(f32[256,3584]{1,0:T(8,128)} %fusion.6, bf16[512,3584]{1,0:T(8,128)(2,1)} %get-tuple-element.15, bf16[256,2048]{1,0:T(8,128)(2,1)S(1)} %copy-done.3, bf16[2048,512]{1,0:T(8,128)(2,1)S(1)} %copy-done.6), kind=kOutput, calls=%fused_computation.4 | convolution fusion | flops 1477443584 | bytes 14155776 | tf_op jit(solution)/shard_map/dot_general | solution.py:25
  174.1 2.9 %dynamic-slice_bitcast_fusion.1 = f32[2,64,3584]{2,1,0:T(8,128)} fusion(f32[2,2,64,3584]{3,2,1,0:T(8,128)} %bitcast.47, s32[]{:T(128)S(6)} %select_n.58), kind=kLoop, calls=%fused_computation.9 | loop fusion | bytes 3670020 | tf_op jit(solution)/shard_map/jit(dynamic_index_in_dim)/squeeze | solution.py:76
  177.4 2.4 bitcast_add_fusion
  179.9 1.6 collective-permute-start.3
  181.5 2.0 bitcast_add_fusion.1
  184.7 1.4 collective-permute-start.1
  186.1 14.7 %add_convert_fusion.2 = bf16[2048,3584]{1,0:T(8,128)(2,1)} fusion(bf16[2048,3584]{1,0:T(8,128)(2,1)} %param.11, bf16[2048,512]{1,0:T(8,128)(2,1)} %get-tuple-element.14, bf16[512,3584]{1,0:T(8,128)(2,1)S(1)} %copy-done.4), kind=kOutput, calls=%fused_computation.2 | convolution fusion | flops 7538212864 | bytes 35127296 | tf_op jit(solution)/shard_map/dot_general | solution.py:25
  200.9 1.6 collective-permute-done.1
  202.6 2.1 constant_dynamic-update-slice_fusion.3
  204.8 1.6 collective-permute-start.5
  206.4 15.4 %add_convert_fusion.1 = bf16[2048,3584]{1,0:T(8,128)(2,1)} fusion(bf16[2048,3584]{1,0:T(8,128)(2,1)} %param.12, bf16[2048,512]{1,0:T(8,128)(2,1)} %get-tuple-element.16, bf16[512,3584]{1,0:T(8,128)(2,1)} %get-tuple-element.17), kind=kOutput, calls=%fused_computation.1 | convolution fusion | flops 7538212864 | bytes 35127296 | tf_op jit(solution)/shard_map/dot_general | solution.py:25
  222.0 1.6 collective-permute-done.6
  223.6 5.8 %fusion = f32[256,2048]{1,0:T(8,128)} fusion(bf16[512,2048]{1,0:T(8,128)(2,1)} %all-gather.2.cloned.1.call-done, bf16[256,3584]{1,0:T(8,128)(2,1)S(1)} %constant_dynamic-update-slice_fusion, bf16[3584,512]{1,0:T(8,128)(2,1)} %get-tuple-element.18), kind=kOutput, calls=%fused_computation.13 | convolution fusion | flops 1476526080 | bytes 9699328 | tf_op jit(solution)/shard_map/dot_general | solution.py:25
  229.4 8.3 %convolution_add_fusion.2 = f32[256,2048]{1,0:T(8,128)S(1)} fusion(f32[256,2048]{1,0:T(8,128)} %fusion, bf16[256,3584]{1,0:T(8,128)(2,1)S(1)} %constant_dynamic-update-slice_fusion, bf16[3584,2048]{1,0:T(8,128)(2,1)} %param.13), kind=kOutput, calls=%fused_computation.5 | convolution fusion | flops 3758620672 | bytes 20709376 | tf_op jit(solution)/shard_map/dot_general | solution.py:25
  237.8 1.3 copy-done.7
  239.3 3.8 %collective-permute-start.9 = (bf16[64,2048]{1,0:T(8,128)(2,1)S(1)}, bf16[64,2048]{1,0:T(8,128)(2,1)S(1)}, u32[]{:S(2)}, u32[]{:S(2)}) collective-permute-start(bf16[64,2048]{1,0:T(8,128)(2,1)S(1)} %get-tuple-element.23), channel_id=1, source_target_pairs={{0,3},{1,0},{2,1},{3,2},{4,7},{5,4},{6,5},{7,6},{8,11},{9,8},{10,9... | collective-permute-start | bytes 786440 | tf_op jit(solution)/shard_map/ppermute | solution.py:92
  243.1 15.3 %add_convert_fusion = bf16[3584,2048]{1,0:T(8,128)(2,1)} fusion(bf16[3584,2048]{1,0:T(8,128)(2,1)} %param.13, bf16[3584,512]{1,0:T(8,128)(2,1)} %get-tuple-element.18, bf16[512,2048]{1,0:T(8,128)(2,1)} %all-gather.2.cloned.1.call-done), kind=kOutput, calls=%fused_computation | convolution fusion | flops 7538212864 | bytes 35127296 | tf_op jit(solution)/shard_map/dot_general | solution.py:25
  258.4 6.4 %collective-permute-done.8 = bf16[64,2048]{1,0:T(8,128)(2,1)S(1)} collective-permute-done((bf16[64,2048]{1,0:T(8,128)(2,1)S(1)}, bf16[64,2048]{1,0:T(8,128)(2,1)S(1)}, u32[]{:S(2)}, u32[]{:S(2)}) %collective-permute-start.8) | collective-permute-done | bytes 262176 | tf_op jit(solution)/shard_map/ppermute | solution.py:92
  264.8 1.9 add_convert_fusion.3
  (40 shorter events, 2.4 us)
Async XLA Ops:
  7.2 216.5 %all-gather.2.cloned.1.call-start = ((), (), s32[]{:S(2)}) async-start(), calls=%async_computation | async-start | bytes 2621440 | tf_op jit(solution)/shard_map/all_gather | solution.py:263
  137.1 11.4 %copy-start.3 = (bf16[256,2048]{1,0:T(8,128)(2,1)S(1)}, bf16[256,2048]{1,0:T(8,128)(2,1)}, u32[]{:S(2)}) copy-start(bf16[256,2048]{1,0:T(8,128)(2,1)} %get-tuple-element.13) | copy-start | bytes 3145732
  137.1 11.4 %copy-start.5 = (bf16[2048,512]{1,0:T(8,128)(2,1)S(1)}, bf16[2048,512]{1,0:T(8,128)(2,1)}, u32[]{:S(2)}) copy-start(bf16[2048,512]{1,0:T(8,128)(2,1)} %get-tuple-element.16) | copy-start | bytes 6291460
  158.2 9.2 %copy-start.6 = (bf16[2048,512]{1,0:T(8,128)(2,1)S(1)}, bf16[2048,512]{1,0:T(8,128)(2,1)}, u32[]{:S(2)}) copy-start(bf16[2048,512]{1,0:T(8,128)(2,1)} %get-tuple-element.14) | copy-start | bytes 6291460
  158.2 19.3 %collective-permute-start.2 = (f32[2,64,3584]{2,1,0:T(8,128)}, f32[2,64,3584]{2,1,0:T(8,128)}, u32[]{:S(2)}, u32[]{:S(2)}) collective-permute-start(f32[2,64,3584]{2,1,0:T(8,128)} %dynamic-slice_bitcast_fusion), channel_id=1, source_target_pairs={{0,4},{4,0},{8,12},{12,8},{1,5},{5,1},{9,13},{13,9},{2,6},{6,2},{1... | collective-permute-start | bytes 5505032 | tf_op jit(solution)/shard_map/ppermute | solution.py:50
  177.0 4.5 %collective-permute-start = (f32[2,64,3584]{2,1,0:T(8,128)}, f32[2,64,3584]{2,1,0:T(8,128)}, u32[]{:S(2)}, u32[]{:S(2)}) collective-permute-start(f32[2,64,3584]{2,1,0:T(8,128)} %dynamic-slice_bitcast_fusion.1), channel_id=1, source_target_pairs={{0,4},{4,0},{8,12},{12,8},{1,5},{5,1},{9,13},{13,9},{2,6},{6,2},{1... | collective-permute-start | bytes 5505032 | tf_op jit(solution)/shard_map/ppermute | solution.py:50
  177.4 4.1 %copy-start = (f32[256,3584]{1,0:T(8,128)S(1)}, f32[256,3584]{1,0:T(8,128)}, u32[]{:S(2)}) copy-start(f32[256,3584]{1,0:T(8,128)} %convolution_add_fusion.1) | copy-start | bytes 11010052
  179.8 3.6 %copy-start.1 = (f32[2,64,3584]{2,1,0:T(8,128)}, f32[2,64,3584]{2,1,0:T(8,128)S(1)}, u32[]{:S(2)}) copy-start(f32[2,64,3584]{2,1,0:T(8,128)S(1)} %bitcast_add_fusion) | copy-start | bytes 5505028
  179.9 6.2 %copy-start.4 = (bf16[512,3584]{1,0:T(8,128)(2,1)S(1)}, bf16[512,3584]{1,0:T(8,128)(2,1)}, u32[]{:S(2)}) copy-start(bf16[512,3584]{1,0:T(8,128)(2,1)} %get-tuple-element.15) | copy-start | bytes 11010052
  179.9 21.0 %collective-permute-start.3 = (bf16[64,3584]{1,0:T(8,128)(2,1)S(1)}, bf16[64,3584]{1,0:T(8,128)(2,1)S(1)}, u32[]{:S(2)}, u32[]{:S(2)}) collective-permute-start(bf16[64,3584]{1,0:T(8,128)(2,1)S(1)} %fusion.4), channel_id=1, source_target_pairs={{0,8},{4,12},{8,0},{12,4},{1,9},{5,13},{9,1},{13,5},{2,10},{6,14},... | collective-permute-start | bytes 1376264 | tf_op jit(solution)/shard_map/ppermute | solution.py:50
  183.5 1.2 copy-start.2
  184.7 17.8 %collective-permute-start.1 = (bf16[64,3584]{1,0:T(8,128)(2,1)S(1)}, bf16[64,3584]{1,0:T(8,128)(2,1)}, u32[]{:S(2)}, u32[]{:S(2)}) collective-permute-start(bf16[64,3584]{1,0:T(8,128)(2,1)S(1)} %fusion.3), channel_id=1, source_target_pairs={{0,8},{4,12},{8,0},{12,4},{1,9},{5,13},{9,1},{13,5},{2,10},{6,14},... | collective-permute-start | bytes 1376264 | tf_op jit(solution)/shard_map/ppermute | solution.py:50
  200.9 1.6 copy-start.8
  204.7 17.2 %collective-permute-start.4 = (bf16[64,3584]{1,0:T(8,128)(2,1)S(1)}, bf16[64,3584]{1,0:T(8,128)(2,1)S(1)}, u32[]{:S(2)}, u32[]{:S(2)}) collective-permute-start(bf16[64,3584]{1,0:T(8,128)(2,1)S(1)} %get-tuple-element.21), channel_id=1, source_target_pairs={{0,4},{4,0},{8,12},{12,8},{1,5},{5,1},{9,13},{13,9},{2,6},{6,2},{1... | collective-permute-start | bytes 1376264 | tf_op jit(solution)/shard_map/ppermute | solution.py:50
  204.8 16.9 %collective-permute-start.5 = (bf16[64,3584]{1,0:T(8,128)(2,1)S(1)}, bf16[64,3584]{1,0:T(8,128)(2,1)S(1)}, u32[]{:S(2)}, u32[]{:S(2)}) collective-permute-start(bf16[64,3584]{1,0:T(8,128)(2,1)S(1)} %get-tuple-element.21), channel_id=1, source_target_pairs={{0,8},{4,12},{8,0},{12,4},{1,9},{5,13},{9,1},{13,5},{2,10},{6,14},... | collective-permute-start | bytes 1376264 | tf_op jit(solution)/shard_map/ppermute | solution.py:50
  221.8 1.8 collective-permute-start.6
  237.7 1.3 copy-start.7
  239.2 19.2 %collective-permute-start.7 = (bf16[64,2048]{1,0:T(8,128)(2,1)S(1)}, bf16[64,2048]{1,0:T(8,128)(2,1)S(1)}, u32[]{:S(2)}, u32[]{:S(2)}) collective-permute-start(bf16[64,2048]{1,0:T(8,128)(2,1)S(1)} %get-tuple-element.22), channel_id=1, source_target_pairs={{0,1},{1,2},{2,3},{3,0},{4,5},{5,6},{6,7},{7,4},{8,9},{9,10},{10,1... | collective-permute-start | bytes 786440 | tf_op jit(solution)/shard_map/ppermute | solution.py:92
  239.3 19.1 %collective-permute-start.9 = (bf16[64,2048]{1,0:T(8,128)(2,1)S(1)}, bf16[64,2048]{1,0:T(8,128)(2,1)S(1)}, u32[]{:S(2)}, u32[]{:S(2)}) collective-permute-start(bf16[64,2048]{1,0:T(8,128)(2,1)S(1)} %get-tuple-element.23), channel_id=1, source_target_pairs={{0,3},{1,0},{2,1},{3,2},{4,7},{5,4},{6,5},{7,6},{8,11},{9,8},{10,9... | collective-permute-start | bytes 786440 | tf_op jit(solution)/shard_map/ppermute | solution.py:92
  243.1 21.7 %collective-permute-start.8 = (bf16[64,2048]{1,0:T(8,128)(2,1)S(1)}, bf16[64,2048]{1,0:T(8,128)(2,1)S(1)}, u32[]{:S(2)}, u32[]{:S(2)}) collective-permute-start(bf16[64,2048]{1,0:T(8,128)(2,1)S(1)} %get-tuple-element.24), channel_id=1, source_target_pairs={{0,2},{1,3},{2,0},{3,1},{4,6},{5,7},{6,4},{7,5},{8,10},{9,11},{10,... | collective-permute-start | bytes 786440 | tf_op jit(solution)/shard_map/ppermute | solution.py:92
Sparse Core Ops, SparseCore 0:
  177.5 44.2 all-gather.1

commit v2 on v1

--- a/solution.py
+++ b/solution.py
@@ -116,7 +116,7 @@
 def gather_kernel(lines, rows, *refs):
     total = len(lines) + len(rows)
     ins, outs = refs[:total], refs[total : 2 * total]
-    own_sem, send_sem, recv_sem = refs[2 * total :]
+    held, (own_sem, send_sem, recv_sem) = refs[2 * total : 3 * total], refs[3 * total :]
     n = 4
     col, row = lax.axis_index("col"), lax.axis_index("row")
     dims = lines + rows
@@ -146,8 +146,11 @@
             device_id_type=pl.DeviceIdType.MESH,
         )
 
-    def own(t):
-        return pltpu.make_async_copy(ins[t], view(t, col if t < len(lines) else row), own_sem.at[t])
+    def load(t):
+        return pltpu.make_async_copy(ins[t], held[t], own_sem.at[t])
+
+    def store(t):
+        return pltpu.make_async_copy(held[t], view(t, col if t < len(lines) else row), own_sem.at[t])
 
     def relay(t, step, way, act):
         slot, target = col - way * step, col + way
@@ -184,7 +187,10 @@
         row_copy(t, 0).start()
         row_copy(t, 1).start()
     for t in range(total):
-        own(t).start()
+        load(t).start()
+    for t in range(total):
+        load(t).wait()
+        store(t).start()
 
     passing = [(t, step) for step in range(1, n) for t in on_line]
     crossing = list(on_row)
@@ -210,7 +216,7 @@
             for step in range(n - 1):
                 relay(t, step, way, "wait")
     for t in range(total):
-        own(t).wait()
+        store(t).wait()
 
 
 def gather_all(nrow, ncol, lines, rows):
@@ -229,14 +235,58 @@
         out_shape=shapes,
         in_specs=[pl.BlockSpec(memory_space=pl.ANY)] * total,
         out_specs=[pl.BlockSpec(memory_space=pl.ANY)] * total,
-        scratch_shapes=[
+        scratch_shapes=[pltpu.VMEM(x.shape, x.dtype) for x, _ in lines + rows]
+        + [
             pltpu.SemaphoreType.DMA((total,)),
             pltpu.SemaphoreType.DMA((total, 6)),
             pltpu.SemaphoreType.DMA((total, 4)),
         ],
-        compiler_params=pltpu.CompilerParams(collective_id=0, has_side_effects=True),
+        compiler_params=pltpu.CompilerParams(collective_id=0, has_side_effects=True, vmem_limit_bytes=60 << 20),
         cost_estimate=pl.CostEstimate(flops=0, bytes_accessed=moved, transcendentals=0),
     )(*[x for x, _ in lines + rows])
+
+
+def merge_apply_kernel(step, x_ref, weight_ref, left_ref, right_ref, merged_ref, out_ref):
+    total = None
+    for start in range(0, weight_ref.shape[0], step):
+        rows = pl.ds(start, step)
+        delta = dot(left_ref[rows, :], right_ref[...])
+        merged = (weight_ref[rows, :].astype(F32) + delta).astype(BF16)
+        merged_ref[rows, :] = merged
+        term = dot(x_ref[:, rows], merged)
+        total = term if total is None else total + term
+    out_ref[...] = total
+
+
+def merge_apply(x, weight, left, right):
+    depth, width = weight.shape
+    tile = 512 if width % 512 == 0 else 128
+    step = 512 if depth % 512 == 0 else depth
+    ranks = left.shape[1]
+    return pl.pallas_call(
+        functools.partial(merge_apply_kernel, step),
+        grid=(width // tile,),
+        in_specs=[
+            pl.BlockSpec(x.shape, lambda j: (0, 0)),
+            pl.BlockSpec((depth, tile), lambda j: (0, j)),
+            pl.BlockSpec((depth, ranks), lambda j: (0, 0)),
+            pl.BlockSpec((ranks, tile), lambda j: (0, j)),
+        ],
+        out_specs=[
+            pl.BlockSpec((depth, tile), lambda j: (0, j)),
+            pl.BlockSpec((x.shape[0], tile), lambda j: (0, j)),
+        ],
+        out_shape=[
+            jax.ShapeDtypeStruct(weight.shape, BF16),
+            jax.ShapeDtypeStruct((x.shape[0], width), F32),
+        ],
+        compiler_params=pltpu.CompilerParams(vmem_limit_bytes=60 << 20),
+        cost_estimate=pl.CostEstimate(
+            flops=2 * depth * width,
+            bytes_accessed=width,
+            transcendentals=0,
+        ),
+    )(x, weight, left, right)
 
 
 def local(
@@ -262,17 +312,13 @@
     down_right, block = lax.optimization_barrier((down_right, block))
     down_r = lax.all_gather(down_right, "col", axis=0, tiled=True)
 
-    def apply(x, weight, left, right):
-        return dot(x, weight) + dot(dot(x, left).astype(BF16), right)
-
-    gate = row_scatter_sum(apply(block, gate_weight, gate_l, gate_r), nrow)
-    up = row_scatter_sum(apply(block, up_weight, up_l, up_r), nrow)
+    gate_merged, gate_terms = merge_apply(block, gate_weight, gate_l, gate_r)
+    gate = row_scatter_sum(gate_terms, nrow)
+    up_merged, up_terms = merge_apply(block, up_weight, up_l, up_r)
+    up = row_scatter_sum(up_terms, nrow)
+    down_merged = merge_delta(down_weight, down_l, down_r)
     hidden = row_gather((jax.nn.silu(gate) * up).astype(BF16), 0, nrow)
-    mixed = col_scatter_sum(apply(hidden, down_weight, down_l, down_r), ncol)
-
-    gate_merged = merge_delta(gate_weight, gate_l, gate_r)
-    up_merged = merge_delta(up_weight, up_l, up_r)
-    down_merged = merge_delta(down_weight, down_l, down_r)
+    mixed = col_scatter_sum(dot(hidden, down_merged), ncol)
     return (mixed.astype(BF16), gate_merged, up_merged, down_merged)
 
 

time: 274 us -> 244 us (0.89)
  matrix products: 93.6 us -> 22.9 us
  waiting for transfers between devices: 9.63 us -> 49.4 us
    dot_general x9 -> x2, matrix products: 93.6 us -> 22.9 us  [dot(): return jnp.dot(a, b, preferred_element_type=F32)]
    pallas_call x1, Pallas kernels: 130 us -> 90.3 us  [gather_all(): pl.pallas_call(functools.partial(gather_kernel, tuple((a for _, a in line...]
    pallas_call x0 -> x2, Pallas kernels: none -> 39.1 us  [merge_apply(): pl.pallas_call(functools.partial(merge_apply_kernel, step), grid=(width /...]
    ppermute x7, waiting for transfers between devices: 3.18 us -> 26.8 us  [row_swap(): return lax.ppermute(x, 'row', [(i, i ^ bit) for i in range(4)])]
    ppermute x3, waiting for transfers between devices: 6.41 us -> 17.4 us  [turn(): return lax.ppermute(x, 'col', [(i, (i + step) % n) for i in range(n)])]
    all_gather x1, waiting for transfers between devices: 0.02 us -> 5.2 us  [local(): down_r = lax.all_gather(down_right, 'col', axis=0, tiled=True)]
  transfers between devices with their start and end apart: 11 -> 11, of which waited for: 3 -> 6; matrix products, arithmetic and copies ran while one was open for 26% -> 11% of each run, Pallas kernels for 0% -> 8%
where the time goes in v2:
time: 244 us; the launch traced here: 241 us
  Pallas kernels  129 us (53%)
  waiting for transfers between devices  49.4 us (20%)
  matrix products  22.9 us (9%)
  between operations  14.2 us (6%)
  local copies, waits for them, and re-layouts  8.95 us (4%)
  starting transfers between devices  8.86 us (4%)
  other arithmetic  7.37 us (3%)
    pallas_call x1, Pallas kernels, gather_all(): pl.pallas_call(functools.partial(gather_kernel, tuple((a for _, a in line...  90.3 us
    pallas_call x2, Pallas kernels, merge_apply(): pl.pallas_call(functools.partial(merge_apply_kernel, step), grid=(width /...  39.1 us
    ppermute x7, waiting for transfers between devices, row_swap(): return lax.ppermute(x, 'row', [(i, i ^ bit) for i in range(4)])  26.8 us
    dot_general x2, matrix products, dot(): return jnp.dot(a, b, preferred_element_type=F32)  22.9 us
    ppermute x3, waiting for transfers between devices, turn(): return lax.ppermute(x, 'col', [(i, (i + step) % n) for i in range(n)])  17.4 us
    all_gather x1, waiting for transfers between devices, local(): down_r = lax.all_gather(down_right, 'col', axis=0, tiled=True)  5.2 us
  transfers between devices with their start and end apart: 11, of which 6 were waited for; matrix products, arithmetic and copies ran while one was open for 11% of the time, Pallas kernels for 8%

profile of v2, /device:TPU:0, one launch (start us, length us, event | category | flops | bytes accessed | tf_op | source)
XLA Modules:
  0.0 241.1 jit_solution(10772041692097039596)
XLA Ops:
  7.2 90.3 %shard_map.129 = (bf16[256,2048]{1,0:T(8,128)(2,1)}, bf16[2048,512]{1,0:T(8,128)(2,1)}, bf16[2048,512]{1,0:T(8,128)(2,1)}, bf16[512,3584]{1,0:T(8,128)(2,1)}, bf...) custom-call(bf16[64,2048]{1,0:T(8,128)(2,1)} %refs_0_.1, bf16[2048,128]{1,0:T(8,128)(2,1)} %refs_1_.1, ...), custom_call_target="tpu_custom_call" | custom-call | bytes 16252928 | tf_op jit(solution)/shard_map/pallas_call | solution.py:233
  97.6 19.5 %shard_map.130 = (bf16[2048,3584]{1,0:T(8,128)(2,1)}, f32[256,3584]{1,0:T(8,128)}) custom-call(bf16[256,2048]{1,0:T(8,128)(2,1)} %get-tuple-element.17.x_ref, bf16[2048,3584]{1,0:T(8,128)(2,1)} %weight_ref.2, bf16[2048,512]{1,0:T(8,128)(2,1)} %get-tuple-element.18.left_ref, bf16[512,3584]{1,0:T(8,128)(2,1)} %get-tuple-element.19.right_ref), custom_call_target="tpu_custom_call" | custom-call | flops 14680064 | bytes 3584 | tf_op jit(solution)/shard_map/pallas_call | solution.py:266
  117.1 1.6 dynamic-slice_bitcast_fusion.1
  118.8 19.5 %shard_map.131 = (bf16[2048,3584]{1,0:T(8,128)(2,1)}, f32[256,3584]{1,0:T(8,128)}) custom-call(bf16[256,2048]{1,0:T(8,128)(2,1)} %get-tuple-element.17.x_ref, bf16[2048,3584]{1,0:T(8,128)(2,1)} %weight_ref.3, bf16[2048,512]{1,0:T(8,128)(2,1)} %get-tuple-element.21.left_ref, bf16[512,3584]{1,0:T(8,128)(2,1)} %get-tuple-element.22.right_ref), custom_call_target="tpu_custom_call" | custom-call | flops 14680064 | bytes 3584 | tf_op jit(solution)/shard_map/pallas_call | solution.py:266
  138.3 2.8 %dynamic-slice_bitcast_fusion = f32[2,64,3584]{2,1,0:T(8,128)} fusion(f32[2,2,64,3584]{3,2,1,0:T(8,128)} %bitcast.30, s32[]{:T(128)S(6)} %select_n.58), kind=kLoop, calls=%fused_computation.3 | loop fusion | bytes 3670020 | tf_op jit(solution)/shard_map/jit(dynamic_index_in_dim)/squeeze | solution.py:76
  141.7 2.4 bitcast_add_fusion.1
  144.2 1.6 collective-permute-start.1
  145.8 1.7 bitcast_add_fusion
  147.5 1.2 copy-done
  148.8 1.2 collective-permute-start.3
  150.0 7.7 %collective-permute-done.1 = bf16[64,3584]{1,0:T(8,128)(2,1)S(1)} collective-permute-done((bf16[64,3584]{1,0:T(8,128)(2,1)S(1)}, bf16[64,3584]{1,0:T(8,128)(2,1)S(1)}, u32[]{:S(2)}, u32[]{:S(2)}) %collective-permute-start.1) | collective-permute-done | bytes 458784 | tf_op jit(solution)/shard_map/ppermute | solution.py:50
  157.6 9.0 %collective-permute-done.3 = bf16[64,3584]{1,0:T(8,128)(2,1)} collective-permute-done((bf16[64,3584]{1,0:T(8,128)(2,1)S(1)}, bf16[64,3584]{1,0:T(8,128)(2,1)}, u32[]{:S(2)}, u32[]{:S(2)}) %collective-permute-start.3) | collective-permute-done | bytes 458784 | tf_op jit(solution)/shard_map/ppermute | solution.py:50
  166.8 1.4 constant_dynamic-update-slice_fusion.3
  168.2 1.2 copy-done.3
  169.4 1.5 collective-permute-start.5
  170.9 10.1 %collective-permute-done.5 = bf16[64,3584]{1,0:T(8,128)(2,1)S(1)} collective-permute-done((bf16[64,3584]{1,0:T(8,128)(2,1)S(1)}, bf16[64,3584]{1,0:T(8,128)(2,1)S(1)}, u32[]{:S(2)}, u32[]{:S(2)}) %collective-permute-start.5) | collective-permute-done | bytes 458784 | tf_op jit(solution)/shard_map/ppermute | solution.py:50
  182.7 5.2 %all-gather.2.cloned.1.call-done = bf16[512,2048]{1,0:T(8,128)(2,1)} async-done(((bf16[128,2048]{1,0:T(8,128)(2,1)}), bf16[512,2048]{1,0:T(8,128)(2,1)}) %all-gather.2.cloned.1.call-update) | async-done | bytes 2097168 | tf_op jit(solution)/shard_map/all_gather | solution.py:313
  187.9 15.4 %add_convert_fusion = bf16[3584,2048]{1,0:T(8,128)(2,1)} fusion(bf16[3584,2048]{1,0:T(8,128)(2,1)} %param.13, bf16[3584,512]{1,0:T(8,128)(2,1)} %get-tuple-element.24, bf16[512,2048]{1,0:T(8,128)(2,1)} %all-gather.2.cloned.1.call-done), kind=kOutput, calls=%fused_computation | convolution fusion | flops 7538212864 | bytes 35127296 | tf_op jit(solution)/shard_map/dot_general | solution.py:25
  203.3 7.5 %fusion.5 = f32[256,2048]{1,0:T(8,128)S(1)} fusion(bf16[256,3584]{1,0:T(8,128)(2,1)S(1)} %constant_dynamic-update-slice_fusion, bf16[3584,2048]{1,0:T(8,128)(2,1)} %add_convert_fusion), kind=kOutput, calls=%fused_computation.21 | convolution fusion | flops 3758096384 | bytes 18612224 | tf_op jit(solution)/shard_map/dot_general | solution.py:25
  211.1 1.7 collective-permute-start.8
  212.7 2.3 collective-permute-start.9
  215.0 7.1 %collective-permute-done.7 = bf16[64,2048]{1,0:T(8,128)(2,1)S(1)} collective-permute-done((bf16[64,2048]{1,0:T(8,128)(2,1)S(1)}, bf16[64,2048]{1,0:T(8,128)(2,1)S(1)}, u32[]{:S(2)}, u32[]{:S(2)}) %collective-permute-start.7) | collective-permute-done | bytes 262176 | tf_op jit(solution)/shard_map/ppermute | solution.py:92
  222.1 10.2 %collective-permute-done.8 = bf16[64,2048]{1,0:T(8,128)(2,1)} collective-permute-done((bf16[64,2048]{1,0:T(8,128)(2,1)S(1)}, bf16[64,2048]{1,0:T(8,128)(2,1)}, u32[]{:S(2)}, u32[]{:S(2)}) %collective-permute-start.8) | collective-permute-done | bytes 262176 | tf_op jit(solution)/shard_map/ppermute | solution.py:92
  232.4 1.9 add_convert_fusion.1
  (27 shorter events, 2.7 us)
Async XLA Ops:
  7.2 180.7 %all-gather.2.cloned.1.call-start = ((), (), s32[]{:S(2)}) async-start(), calls=%async_computation | async-start | bytes 2621440 | tf_op jit(solution)/shard_map/all_gather | solution.py:313
  118.7 23.0 %collective-permute-start = (f32[2,64,3584]{2,1,0:T(8,128)S(1)}, f32[2,64,3584]{2,1,0:T(8,128)}, u32[]{:S(2)}, u32[]{:S(2)}) collective-permute-start(f32[2,64,3584]{2,1,0:T(8,128)S(1)} %dynamic-slice_bitcast_fusion.1), channel_id=1, source_target_pairs={{0,4},{4,0},{8,12},{12,8},{1,5},{5,1},{9,13},{13,9},{2,6},{6,2},{1... | collective-permute-start | bytes 5505032 | tf_op jit(solution)/shard_map/ppermute | solution.py:50
  141.2 4.6 %collective-permute-start.2 = (f32[2,64,3584]{2,1,0:T(8,128)}, f32[2,64,3584]{2,1,0:T(8,128)}, u32[]{:S(2)}, u32[]{:S(2)}) collective-permute-start(f32[2,64,3584]{2,1,0:T(8,128)} %dynamic-slice_bitcast_fusion), channel_id=1, source_target_pairs={{0,4},{4,0},{8,12},{12,8},{1,5},{5,1},{9,13},{13,9},{2,6},{6,2},{1... | collective-permute-start | bytes 5505032 | tf_op jit(solution)/shard_map/ppermute | solution.py:50
  141.7 4.1 %copy-start.2 = (f32[256,3584]{1,0:T(8,128)S(1)}, f32[256,3584]{1,0:T(8,128)}, u32[]{:S(2)}) copy-start(f32[256,3584]{1,0:T(8,128)} %get-tuple-element.23) | copy-start | bytes 11010052
  144.2 13.4 %collective-permute-start.1 = (bf16[64,3584]{1,0:T(8,128)(2,1)S(1)}, bf16[64,3584]{1,0:T(8,128)(2,1)S(1)}, u32[]{:S(2)}, u32[]{:S(2)}) collective-permute-start(bf16[64,3584]{1,0:T(8,128)(2,1)S(1)} %fusion.2), channel_id=1, source_target_pairs={{0,8},{4,12},{8,0},{12,4},{1,9},{5,13},{9,1},{13,5},{2,10},{6,14},... | collective-permute-start | bytes 1376264 | tf_op jit(solution)/shard_map/ppermute | solution.py:50
  147.5 1.2 copy-start
  148.8 17.9 %collective-permute-start.3 = (bf16[64,3584]{1,0:T(8,128)(2,1)S(1)}, bf16[64,3584]{1,0:T(8,128)(2,1)}, u32[]{:S(2)}, u32[]{:S(2)}) collective-permute-start(bf16[64,3584]{1,0:T(8,128)(2,1)S(1)} %fusion.3), channel_id=1, source_target_pairs={{0,8},{4,12},{8,0},{12,4},{1,9},{5,13},{9,1},{13,5},{2,10},{6,14},... | collective-permute-start | bytes 1376264 | tf_op jit(solution)/shard_map/ppermute | solution.py:50
  150.0 16.8 %copy-start.1 = (f32[2,64,3584]{2,1,0:T(8,128)S(1)}, f32[2,64,3584]{2,1,0:T(8,128)}, u32[]{:S(2)}) copy-start(f32[2,64,3584]{2,1,0:T(8,128)} %copy-done) | copy-start | bytes 5505028
  168.2 1.3 copy-start.3
  169.4 11.6 %collective-permute-start.5 = (bf16[64,3584]{1,0:T(8,128)(2,1)S(1)}, bf16[64,3584]{1,0:T(8,128)(2,1)S(1)}, u32[]{:S(2)}, u32[]{:S(2)}) collective-permute-start(bf16[64,3584]{1,0:T(8,128)(2,1)S(1)} %get-tuple-element.29), channel_id=1, source_target_pairs={{0,8},{4,12},{8,0},{12,4},{1,9},{5,13},{9,1},{13,5},{2,10},{6,14},... | collective-permute-start | bytes 1376264 | tf_op jit(solution)/shard_map/ppermute | solution.py:50
  170.9 10.1 %collective-permute-start.4 = (bf16[64,3584]{1,0:T(8,128)(2,1)S(1)}, bf16[64,3584]{1,0:T(8,128)(2,1)S(1)}, u32[]{:S(2)}, u32[]{:S(2)}) collective-permute-start(bf16[64,3584]{1,0:T(8,128)(2,1)S(1)} %get-tuple-element.29), channel_id=1, source_target_pairs={{0,4},{4,0},{8,12},{12,8},{1,5},{5,1},{9,13},{13,9},{2,6},{6,2},{1... | collective-permute-start | bytes 1376264 | tf_op jit(solution)/shard_map/ppermute | solution.py:50
  181.0 22.2 %collective-permute-start.6 = (bf16[64,3584]{1,0:T(8,128)(2,1)S(1)}, bf16[64,3584]{1,0:T(8,128)(2,1)S(1)}, u32[]{:S(2)}, u32[]{:S(2)}) collective-permute-start(bf16[64,3584]{1,0:T(8,128)(2,1)S(1)} %collective-permute-done.5), channel_id=1, source_target_pairs={{0,4},{4,0},{8,12},{12,8},{1,5},{5,1},{9,13},{13,9},{2,6},{6,2},{1... | collective-permute-start | bytes 1376264 | tf_op jit(solution)/shard_map/ppermute | solution.py:50
  187.9 15.4 %copy-start.4 = (bf16[256,3584]{1,0:T(8,128)(2,1)S(1)}, bf16[256,3584]{1,0:T(8,128)(2,1)}, u32[]{:S(2)}) copy-start(bf16[256,3584]{1,0:T(8,128)(2,1)} %constant_dynamic-update-slice_fusion.1) | copy-start | bytes 5505028
  211.0 11.1 %collective-permute-start.7 = (bf16[64,2048]{1,0:T(8,128)(2,1)S(1)}, bf16[64,2048]{1,0:T(8,128)(2,1)S(1)}, u32[]{:S(2)}, u32[]{:S(2)}) collective-permute-start(bf16[64,2048]{1,0:T(8,128)(2,1)S(1)} %get-tuple-element.30), channel_id=1, source_target_pairs={{0,1},{1,2},{2,3},{3,0},{4,5},{5,6},{6,7},{7,4},{8,9},{9,10},{10,1... | collective-permute-start | bytes 786440 | tf_op jit(solution)/shard_map/ppermute | solution.py:92
  211.1 21.3 %collective-permute-start.8 = (bf16[64,2048]{1,0:T(8,128)(2,1)S(1)}, bf16[64,2048]{1,0:T(8,128)(2,1)}, u32[]{:S(2)}, u32[]{:S(2)}) collective-permute-start(bf16[64,2048]{1,0:T(8,128)(2,1)S(1)} %get-tuple-element.32), channel_id=1, source_target_pairs={{0,2},{1,3},{2,0},{3,1},{4,6},{5,7},{6,4},{7,5},{8,10},{9,11},{10,... | collective-permute-start | bytes 786440 | tf_op jit(solution)/shard_map/ppermute | solution.py:92
  212.7 19.6 %collective-permute-start.9 = (bf16[64,2048]{1,0:T(8,128)(2,1)S(1)}, bf16[64,2048]{1,0:T(8,128)(2,1)}, u32[]{:S(2)}, u32[]{:S(2)}) collective-permute-start(bf16[64,2048]{1,0:T(8,128)(2,1)S(1)} %get-tuple-element.31), channel_id=1, source_target_pairs={{0,3},{1,0},{2,1},{3,2},{4,7},{5,4},{6,5},{7,6},{8,11},{9,8},{10,9... | collective-permute-start | bytes 786440 | tf_op jit(solution)/shard_map/ppermute | solution.py:92
Sparse Core Ops, SparseCore 0:
  141.8 46.0 all-gather.1

commit v3 on v2

--- a/solution.py
+++ b/solution.py
@@ -23,10 +23,6 @@
 
 def dot(a, b):
     return jnp.dot(a, b, preferred_element_type=F32)
-
-
-def merge_delta(weight, left, right):
-    return (weight.astype(F32) + dot(left, right)).astype(BF16)
 
 
 def line_gather(x, axis, n):
@@ -316,9 +312,9 @@
     gate = row_scatter_sum(gate_terms, nrow)
     up_merged, up_terms = merge_apply(block, up_weight, up_l, up_r)
     up = row_scatter_sum(up_terms, nrow)
-    down_merged = merge_delta(down_weight, down_l, down_r)
     hidden = row_gather((jax.nn.silu(gate) * up).astype(BF16), 0, nrow)
-    mixed = col_scatter_sum(dot(hidden, down_merged), ncol)
+    down_merged, down_terms = merge_apply(hidden, down_weight, down_l, down_r)
+    mixed = col_scatter_sum(down_terms, ncol)
     return (mixed.astype(BF16), gate_merged, up_merged, down_merged)
 
 

time: 244 us -> 251 us (1.029)
  matrix products: 22.9 us -> 0 us
  Pallas kernels: 129 us -> 149 us
  waiting for transfers between devices: 49.4 us -> 59.3 us
    dot_general x2 -> x0, matrix products: 22.9 us -> none  [dot(): return jnp.dot(a, b, preferred_element_type=F32)]
    pallas_call x2 -> x3, Pallas kernels: 39.1 us -> 58.7 us  [merge_apply(): pl.pallas_call(functools.partial(merge_apply_kernel, step), grid=(width /...]
    all_gather x1, waiting for transfers between devices: 5.2 us -> 13.9 us  [local(): down_r = lax.all_gather(down_right, 'col', axis=0, tiled=True)]
  transfers between devices with their start and end apart: 11 -> 11, of which waited for: 6 -> 8; matrix products, arithmetic and copies ran while one was open for 11% -> 3% of each run, Pallas kernels for 8% -> 8%
where the time goes in v3:
time: 251 us; the launch traced here: 248 us
  Pallas kernels  149 us (59%)
  waiting for transfers between devices  59.3 us (24%)
  between operations  14.2 us (6%)
  starting transfers between devices  9.2 us (4%)
  local copies, waits for them, and re-layouts  8.82 us (4%)
  other arithmetic  7 us (3%)
    pallas_call x1, Pallas kernels, gather_all(): pl.pallas_call(functools.partial(gather_kernel, tuple((a for _, a in line...  90.3 us
    pallas_call x3, Pallas kernels, merge_apply(): pl.pallas_call(functools.partial(merge_apply_kernel, step), grid=(width /...  58.7 us
    ppermute x7, waiting for transfers between devices, row_swap(): return lax.ppermute(x, 'row', [(i, i ^ bit) for i in range(4)])  28.2 us
    ppermute x3, waiting for transfers between devices, turn(): return lax.ppermute(x, 'col', [(i, (i + step) % n) for i in range(n)])  17.2 us
    all_gather x1, waiting for transfers between devices, local(): down_r = lax.all_gather(down_right, 'col', axis=0, tiled=True)  13.9 us
    squeeze x2, local copies, waits for them, and re-layouts, row_scatter_sum(): given = lax.dynamic_index_in_dim(blocks, 1 - core, 1, keepdims=False)  5.85 us
    ppermute x7, starting transfers between devices, row_swap(): return lax.ppermute(x, 'row', [(i, i ^ bit) for i in range(4)])  5.12 us
  transfers between devices with their start and end apart: 11, of which 8 were waited for; matrix products, arithmetic and copies ran while one was open for 3% of the time, Pallas kernels for 8%

profile of v3, /device:TPU:0, one launch (start us, length us, event | category | flops | bytes accessed | tf_op | source)
XLA Modules:
  0.0 247.6 jit_solution(15307996259792992728)
XLA Ops:
  7.2 90.3 %shard_map.129 = (bf16[256,2048]{1,0:T(8,128)(2,1)}, bf16[2048,512]{1,0:T(8,128)(2,1)}, bf16[2048,512]{1,0:T(8,128)(2,1)}, bf16[512,3584]{1,0:T(8,128)(2,1)}, bf...) custom-call(bf16[64,2048]{1,0:T(8,128)(2,1)} %refs_0_.1, bf16[2048,128]{1,0:T(8,128)(2,1)} %refs_1_.1, ...), custom_call_target="tpu_custom_call" | custom-call | bytes 16252928 | tf_op jit(solution)/shard_map/pallas_call | solution.py:229
  97.6 19.5 %shard_map.130 = (bf16[2048,3584]{1,0:T(8,128)(2,1)}, f32[256,3584]{1,0:T(8,128)}) custom-call(bf16[256,2048]{1,0:T(8,128)(2,1)} %get-tuple-element.19.x_ref, bf16[2048,3584]{1,0:T(8,128)(2,1)} %weight_ref.3, bf16[2048,512]{1,0:T(8,128)(2,1)} %get-tuple-element.20.left_ref, bf16[512,3584]{1,0:T(8,128)(2,1)} %get-tuple-element.21.right_ref), custom_call_target="tpu_custom_call" | custom-call | flops 14680064 | bytes 3584 | tf_op jit(solution)/shard_map/pallas_call | solution.py:262
  117.1 2.9 %dynamic-slice_bitcast_fusion.1 = f32[2,64,3584]{2,1,0:T(8,128)} fusion(f32[2,2,64,3584]{3,2,1,0:T(8,128)} %bitcast.36, s32[]{:T(128)S(6)} %select_n.58), kind=kLoop, calls=%fused_computation.3 | loop fusion | bytes 3670020 | tf_op jit(solution)/shard_map/jit(dynamic_index_in_dim)/squeeze | solution.py:72
  120.0 19.5 %shard_map.131 = (bf16[2048,3584]{1,0:T(8,128)(2,1)}, f32[256,3584]{1,0:T(8,128)}) custom-call(bf16[256,2048]{1,0:T(8,128)(2,1)} %get-tuple-element.19.x_ref, bf16[2048,3584]{1,0:T(8,128)(2,1)} %weight_ref.4, bf16[2048,512]{1,0:T(8,128)(2,1)} %get-tuple-element.23.left_ref, bf16[512,3584]{1,0:T(8,128)(2,1)} %get-tuple-element.24.right_ref), custom_call_target="tpu_custom_call" | custom-call | flops 14680064 | bytes 3584 | tf_op jit(solution)/shard_map/pallas_call | solution.py:262
  139.5 2.9 %dynamic-slice_bitcast_fusion = f32[2,64,3584]{2,1,0:T(8,128)} fusion(f32[2,2,64,3584]{3,2,1,0:T(8,128)} %bitcast.34, s32[]{:T(128)S(6)} %select_n.58), kind=kLoop, calls=%fused_computation.2 | loop fusion | bytes 3670020 | tf_op jit(solution)/shard_map/jit(dynamic_index_in_dim)/squeeze | solution.py:72
  143.0 1.8 bitcast_add_fusion.1
  144.9 1.6 collective-permute-start.1
  146.7 1.7 bitcast_add_fusion
  148.5 1.2 copy-done.3
  149.7 1.5 collective-permute-start.3
  151.2 7.1 %collective-permute-done.1 = bf16[64,3584]{1,0:T(8,128)(2,1)S(1)} collective-permute-done((bf16[64,3584]{1,0:T(8,128)(2,1)S(1)}, bf16[64,3584]{1,0:T(8,128)(2,1)S(1)}, u32[]{:S(2)}, u32[]{:S(2)}) %collective-permute-start.1) | collective-permute-done | bytes 458784 | tf_op jit(solution)/shard_map/ppermute | solution.py:46
  158.3 8.9 %collective-permute-done.3 = bf16[64,3584]{1,0:T(8,128)(2,1)S(1)} collective-permute-done((bf16[64,3584]{1,0:T(8,128)(2,1)S(1)}, bf16[64,3584]{1,0:T(8,128)(2,1)S(1)}, u32[]{:S(2)}, u32[]{:S(2)}) %collective-permute-start.3) | collective-permute-done | bytes 458784 | tf_op jit(solution)/shard_map/ppermute | solution.py:46
  167.4 1.6 constant_dynamic-update-slice_fusion.3
  168.9 1.6 collective-permute-start.5
  170.5 10.2 %collective-permute-done.5 = bf16[64,3584]{1,0:T(8,128)(2,1)S(1)} collective-permute-done((bf16[64,3584]{1,0:T(8,128)(2,1)S(1)}, bf16[64,3584]{1,0:T(8,128)(2,1)S(1)}, u32[]{:S(2)}, u32[]{:S(2)}) %collective-permute-start.5) | collective-permute-done | bytes 458784 | tf_op jit(solution)/shard_map/ppermute | solution.py:46
  180.8 1.7 collective-permute-done.6
  182.6 13.9 %all-gather.2.cloned.1.call-done.right_ref = bf16[512,2048]{1,0:T(8,128)(2,1)} async-done(((bf16[128,2048]{1,0:T(8,128)(2,1)}), bf16[512,2048]{1,0:T(8,128)(2,1)}) %all-gather.2.cloned.1.call-update) | async-done | bytes 2097168 | tf_op jit(solution)/shard_map/all_gather | solution.py:309
  196.5 19.6 %shard_map.132 = (bf16[3584,2048]{1,0:T(8,128)(2,1)}, f32[256,2048]{1,0:T(8,128)}) custom-call(bf16[256,3584]{1,0:T(8,128)(2,1)} %copy-done, bf16[3584,2048]{1,0:T(8,128)(2,1)} %weight_ref.5, bf16[3584,512]{1,0:T(8,128)(2,1)} %get-tuple-element.26.left_ref, bf16[512,2048]{1,0:T(8,128)(2,1)} %all-gather.2.cloned.1.call-done.right_ref), custom_call_target="tpu_custom_call" | custom-call | flops 14680064 | bytes 2048 | tf_op jit(solution)/shard_map/pallas_call | solution.py:262
  216.1 1.5 dynamic-slice_convert_fusion.4
  217.6 1.7 collective-permute-start.8
  219.4 2.3 collective-permute-start.9
  221.6 7.1 %collective-permute-done.7 = bf16[64,2048]{1,0:T(8,128)(2,1)S(1)} collective-permute-done((bf16[64,2048]{1,0:T(8,128)(2,1)S(1)}, bf16[64,2048]{1,0:T(8,128)(2,1)S(1)}, u32[]{:S(2)}, u32[]{:S(2)}) %collective-permute-start.7) | collective-permute-done | bytes 262176 | tf_op jit(solution)/shard_map/ppermute | solution.py:88
  228.7 10.1 %collective-permute-done.8 = bf16[64,2048]{1,0:T(8,128)(2,1)S(1)} collective-permute-done((bf16[64,2048]{1,0:T(8,128)(2,1)S(1)}, bf16[64,2048]{1,0:T(8,128)(2,1)S(1)}, u32[]{:S(2)}, u32[]{:S(2)}) %collective-permute-start.8) | collective-permute-done | bytes 262176 | tf_op jit(solution)/shard_map/ppermute | solution.py:88
  238.9 1.9 add_convert_fusion
  (26 shorter events, 1.3 us)
Async XLA Ops:
  7.2 189.3 %all-gather.2.cloned.1.call-start = ((), (), s32[]{:S(2)}) async-start(), calls=%async_computation | async-start | bytes 2621440 | tf_op jit(solution)/shard_map/all_gather | solution.py:309
  120.0 22.9 %collective-permute-start = (f32[2,64,3584]{2,1,0:T(8,128)}, f32[2,64,3584]{2,1,0:T(8,128)S(1)}, u32[]{:S(2)}, u32[]{:S(2)}) collective-permute-start(f32[2,64,3584]{2,1,0:T(8,128)} %dynamic-slice_bitcast_fusion.1), channel_id=1, source_target_pairs={{0,4},{4,0},{8,12},{12,8},{1,5},{5,1},{9,13},{13,9},{2,6},{6,2},{1... | collective-permute-start | bytes 5505032 | tf_op jit(solution)/shard_map/ppermute | solution.py:46
  142.5 4.3 %collective-permute-start.2 = (f32[2,64,3584]{2,1,0:T(8,128)}, f32[2,64,3584]{2,1,0:T(8,128)}, u32[]{:S(2)}, u32[]{:S(2)}) collective-permute-start(f32[2,64,3584]{2,1,0:T(8,128)} %dynamic-slice_bitcast_fusion), channel_id=1, source_target_pairs={{0,4},{4,0},{8,12},{12,8},{1,5},{5,1},{9,13},{13,9},{2,6},{6,2},{1... | collective-permute-start | bytes 5505032 | tf_op jit(solution)/shard_map/ppermute | solution.py:46
  143.0 3.8 %copy-start.4 = (f32[256,3584]{1,0:T(8,128)S(1)}, f32[256,3584]{1,0:T(8,128)}, u32[]{:S(2)}) copy-start(f32[256,3584]{1,0:T(8,128)} %get-tuple-element.25) | copy-start | bytes 11010052
  144.8 3.6 %copy-start.1 = (f32[2,64,3584]{2,1,0:T(8,128)}, f32[2,64,3584]{2,1,0:T(8,128)S(1)}, u32[]{:S(2)}) copy-start(f32[2,64,3584]{2,1,0:T(8,128)S(1)} %bitcast_add_fusion.1) | copy-start | bytes 5505028
  144.9 13.4 %collective-permute-start.1 = (bf16[64,3584]{1,0:T(8,128)(2,1)S(1)}, bf16[64,3584]{1,0:T(8,128)(2,1)S(1)}, u32[]{:S(2)}, u32[]{:S(2)}) collective-permute-start(bf16[64,3584]{1,0:T(8,128)(2,1)S(1)} %fusion.2), channel_id=1, source_target_pairs={{0,8},{4,12},{8,0},{12,4},{1,9},{5,13},{9,1},{13,5},{2,10},{6,14},... | collective-permute-start | bytes 1376264 | tf_op jit(solution)/shard_map/ppermute | solution.py:46
  148.5 1.2 copy-start.3
  149.7 17.5 %collective-permute-start.3 = (bf16[64,3584]{1,0:T(8,128)(2,1)S(1)}, bf16[64,3584]{1,0:T(8,128)(2,1)S(1)}, u32[]{:S(2)}, u32[]{:S(2)}) collective-permute-start(bf16[64,3584]{1,0:T(8,128)(2,1)S(1)} %fusion.3), channel_id=1, source_target_pairs={{0,8},{4,12},{8,0},{12,4},{1,9},{5,13},{9,1},{13,5},{2,10},{6,14},... | collective-permute-start | bytes 1376264 | tf_op jit(solution)/shard_map/ppermute | solution.py:46
  151.2 16.1 %copy-start.2 = (f32[2,64,3584]{2,1,0:T(8,128)S(1)}, f32[2,64,3584]{2,1,0:T(8,128)}, u32[]{:S(2)}) copy-start(f32[2,64,3584]{2,1,0:T(8,128)} %copy-done.1) | copy-start | bytes 5505028
  168.9 11.8 %collective-permute-start.5 = (bf16[64,3584]{1,0:T(8,128)(2,1)S(1)}, bf16[64,3584]{1,0:T(8,128)(2,1)S(1)}, u32[]{:S(2)}, u32[]{:S(2)}) collective-permute-start(bf16[64,3584]{1,0:T(8,128)(2,1)S(1)} %get-tuple-element.33), channel_id=1, source_target_pairs={{0,8},{4,12},{8,0},{12,4},{1,9},{5,13},{9,1},{13,5},{2,10},{6,14},... | collective-permute-start | bytes 1376264 | tf_op jit(solution)/shard_map/ppermute | solution.py:46
  170.5 10.2 %collective-permute-start.4 = (bf16[64,3584]{1,0:T(8,128)(2,1)S(1)}, bf16[64,3584]{1,0:T(8,128)(2,1)S(1)}, u32[]{:S(2)}, u32[]{:S(2)}) collective-permute-start(bf16[64,3584]{1,0:T(8,128)(2,1)S(1)} %get-tuple-element.33), channel_id=1, source_target_pairs={{0,4},{4,0},{8,12},{12,8},{1,5},{5,1},{9,13},{13,9},{2,6},{6,2},{1... | collective-permute-start | bytes 1376264 | tf_op jit(solution)/shard_map/ppermute | solution.py:46
  180.7 1.8 collective-permute-start.6
  182.5 13.9 %copy-start = (bf16[256,3584]{1,0:T(8,128)(2,1)}, bf16[256,3584]{1,0:T(8,128)(2,1)S(1)}, u32[]{:S(2)}) copy-start(bf16[256,3584]{1,0:T(8,128)(2,1)S(1)} %constant_dynamic-update-slice_fusion.x_ref) | copy-start | bytes 5505028
  217.6 11.1 %collective-permute-start.7 = (bf16[64,2048]{1,0:T(8,128)(2,1)S(1)}, bf16[64,2048]{1,0:T(8,128)(2,1)S(1)}, u32[]{:S(2)}, u32[]{:S(2)}) collective-permute-start(bf16[64,2048]{1,0:T(8,128)(2,1)S(1)} %get-tuple-element.34), channel_id=1, source_target_pairs={{0,1},{1,2},{2,3},{3,0},{4,5},{5,6},{6,7},{7,4},{8,9},{9,10},{10,1... | collective-permute-start | bytes 786440 | tf_op jit(solution)/shard_map/ppermute | solution.py:88
  217.6 21.2 %collective-permute-start.8 = (bf16[64,2048]{1,0:T(8,128)(2,1)S(1)}, bf16[64,2048]{1,0:T(8,128)(2,1)S(1)}, u32[]{:S(2)}, u32[]{:S(2)}) collective-permute-start(bf16[64,2048]{1,0:T(8,128)(2,1)S(1)} %get-tuple-element.36), channel_id=1, source_target_pairs={{0,2},{1,3},{2,0},{3,1},{4,6},{5,7},{6,4},{7,5},{8,10},{9,11},{10,... | collective-permute-start | bytes 786440 | tf_op jit(solution)/shard_map/ppermute | solution.py:88
  219.4 19.5 %collective-permute-start.9 = (bf16[64,2048]{1,0:T(8,128)(2,1)S(1)}, bf16[64,2048]{1,0:T(8,128)(2,1)S(1)}, u32[]{:S(2)}, u32[]{:S(2)}) collective-permute-start(bf16[64,2048]{1,0:T(8,128)(2,1)S(1)} %get-tuple-element.35), channel_id=1, source_target_pairs={{0,3},{1,0},{2,1},{3,2},{4,7},{5,4},{6,5},{7,6},{8,11},{9,8},{10,9... | collective-permute-start | bytes 786440 | tf_op jit(solution)/shard_map/ppermute | solution.py:88
Sparse Core Ops, SparseCore 0:
  151.3 45.0 all-gather.1
